TPU v7x, 128 devices: a whole 4x4x4 slice. The times are simulated.
128 devices in a mesh: dp: 32 (over x_lo, z, y), section: 4 (over x_hi, core).
Axes of the slice: x: 4 (x_hi: 2, x_lo: 2; x = x_hi * 2 + x_lo), y: 4, z: 4, core: 2. Of those that a mesh axis runs over, the one named last changes fastest.
Arguments:
- canvas_in: bfloat16 [64, 400, 1152], P('dp', None, 'section'), may hold values from -6 to 6
- conditioning: bfloat16 [64, 1152], P('dp'), may hold values from -6 to 6
- grid_shape: int32 [64], P('dp'), may hold values from 0 to 2, as said below
- kept_rank: int32 [64, 128], P('dp'), may hold values from 0 to 255, as said below
- first_weight: bfloat16 [4, 1152, 4608], P('section')
- second_weight: bfloat16 [4, 4608, 1152], P('section')
- modulation_weight: bfloat16 [4, 1152, 3456], P('section')
- modulation_bias: float32 [4, 3456], P('section'), may hold values from -3 to 3
- out_grad: bfloat16 [64, 400, 1152], P('dp', None, 'section'), may hold values from -6 to 6
Outputs:
- result: bfloat16 [64, 400, 1152], P('dp', None, 'section')
- canvas_grad: bfloat16 [64, 400, 1152], P('dp', None, 'section')
- first_grad: float32 [4, 1152, 4608], P('section', None, 'dp')
- second_grad: float32 [4, 4608, 1152], P('section', 'dp')
- modulation_grad: float32 [4, 1152, 3456], P('section')
- bias_grad: float32 [4, 3456], P('section')
Inputs may be any that keep to these rules, and one draw needn't show every extreme that they name: `grid_shape`: 0, 1 or 2 for each canvas. `kept_rank`: each row holds 128 different token numbers in increasing order, all below the number of real tokens of its canvas.
All inputs are finite; a program needn't handle non-finite values.
Results may differ from a plain program's by a relative error of at most 0.025.
Values may be sent and summed in bfloat16 or wider, within the bound.
A program may use at most 384 MiB of HBM per device.

v0:
```python
import functools
import math

import jax
import jax.numpy as jnp
from jax import lax
from jax.experimental import pallas as pl
from jax.experimental.pallas import tpu as pltpu
from jax.sharding import PartitionSpec as P

HEADS = 16
SIDE = 20
SLOTS = SIDE * SIDE
VALID = 256
KEPT = 128
D = 1152
FF = 4608
HALF = FF // 2
QUARTER = D // 4
WINDOW = 384
PACKED = 80
EARLY = 512
HEAD = D // HEADS
BLOCK = FF // 32
EPSILON = 1e-06
FACTOR = 1.0 / math.sqrt(HEAD)
LOG2E = math.log2(math.e)
NEGATIVE = -1e30
BF = jnp.bfloat16
F32 = jnp.float32
VMEM = pltpu.VMEM
MESH = pl.DeviceIdType.MESH
NT = (((1,), (1,)), ((), ()))
TN = (((0,), (0,)), ((), ()))
C0 = math.sqrt(2.0 / math.pi)


def mm(a, b, dims=(((1,), (0,)), ((), ()))):
    return lax.dot_general(a, b, dims, preferred_element_type=F32)


def cost(flops, nbytes):
    return pl.CostEstimate(flops=int(flops), bytes_accessed=int(nbytes), transcendentals=0)


def array(*shape, dtype=BF):
    return jax.ShapeDtypeStruct(shape, dtype)


def norm_stats(x):
    mean = jnp.mean(x, axis=-1, keepdims=True)
    centred = x - mean
    rstd = lax.rsqrt(jnp.mean(centred * centred, axis=-1, keepdims=True) + EPSILON)
    return centred * rstd, rstd


def norm_forward(rows, shift, scale):
    normed, _ = norm_stats(rows)
    return (normed * (1.0 + scale) + shift).astype(BF)


def norm_backward(rows, scale, upstream, hidden_grad):
    normed, rstd = norm_stats(rows)
    shift_grad = jnp.sum(hidden_grad, axis=0, keepdims=True)
    scale_grad = jnp.sum(hidden_grad * normed, axis=0, keepdims=True)
    scaled = hidden_grad * (1.0 + scale)
    mean_scaled = jnp.mean(scaled, axis=-1, keepdims=True)
    mean_product = jnp.mean(scaled * normed, axis=-1, keepdims=True)
    grad = upstream + (scaled - mean_scaled - normed * mean_product) * rstd
    return grad.astype(BF), shift_grad, scale_grad


def gelu_pair(v):
    square = v * v
    t = jnp.tanh(v * (C0 + (C0 * 0.044715) * square))
    half = 0.5 * (1.0 + t)
    slope = half + (0.5 * v) * (1.0 - t * t) * (C0 + (3.0 * C0 * 0.044715) * square)
    return v * half, slope


def kept_spread(kept_row):
    line = lax.broadcasted_iota(jnp.int32, (VALID, KEPT), 0)
    return (line == kept_row).astype(F32)


def pick_kept(rows, kept_row):
    return mm(kept_spread(kept_row).astype(BF), rows, TN).astype(BF)


def merge_kept(base, kept_rows, kept_row):
    spread = kept_spread(kept_row)
    chosen = jnp.sum(spread, axis=1, keepdims=True) > 0.5
    return jnp.where(chosen, mm(spread.astype(BF), kept_rows).astype(BF), base)


def grid_of(shape_id):
    lines = jnp.where(shape_id == 1, 12, jnp.where(shape_id == 2, 20, 16))
    width = jnp.where(shape_id == 1, 20, jnp.where(shape_id == 2, 12, 16))
    return lines, width


def slots_of_tokens(shape_id):
    lines, width = grid_of(shape_id)
    slot = lax.broadcasted_iota(jnp.int32, (1, SLOTS), 1)
    line = (slot * 3277) >> 16
    column = slot - line * SIDE
    token = jnp.where((line < lines) & (column < width), line * width + column, -1)
    return (lax.broadcasted_iota(jnp.int32, (VALID, SLOTS), 0) == token).astype(BF)


def shift_matrix(section):
    line = lax.broadcasted_iota(jnp.int32, (QUARTER, WINDOW), 0)
    lane = lax.broadcasted_iota(jnp.int32, (QUARTER, WINDOW), 1)
    return (lane == line + 32 * section).astype(BF)


HEADS_OF_GROUP = ((0, 0), (0, 72), (128, 16), (128, 88))


def overlaid(parts):
    first, last = parts[0] + parts[1], parts[2] + parts[3]
    return jnp.concatenate([first[:, 0:128], first[:, 128:256] + last[:, 0:128], last[:, 128:256]], axis=1)


def only_head(value, offset):
    lane = lax.broadcasted_iota(jnp.int32, value.shape, 1)
    return jnp.where((lane >= offset) & (lane < offset + HEAD), value, jnp.zeros_like(value))


def key_bias(live, keys):
    lane = lax.broadcasted_iota(jnp.int32, (1, keys), 1)
    return jnp.where(lane < live, 0.0, NEGATIVE).astype(F32)


def softmax_of(q, k, bias):
    scores = mm(q, k, NT)
    if bias is not None:
        scores = scores + bias
    top = jnp.max(scores, axis=-1, keepdims=True)
    grown = jnp.exp2((scores - top) * (FACTOR * LOG2E))
    return grown * (1.0 / jnp.sum(grown, axis=-1, keepdims=True))


class Copies:
    def __init__(self, send, arrive):
        self.send, self.arrive, self.first, self.size = send, arrive, {}, 0

    def name(self, key, count):
        self.first[key] = self.size
        self.size += count

    def remote(self, key, index, source, target, device, sender=None):
        at = self.first[key]
        return pltpu.make_async_remote_copy(
            src_ref=source,
            dst_ref=target,
            send_sem=self.send.at[at + (index if sender is None else sender)],
            recv_sem=self.arrive.at[at + index],
            device_id=device,
            device_id_type=MESH,
        )

    def local(self, key, index, source, target):
        return pltpu.make_async_copy(source, target, self.send.at[self.first[key] + index])


PIPE_COPIES = (
    ("wm", 3), ("w1", 2), ("w2", 2), ("in", 8), ("og", 16), ("forward", 2), ("done", 2), ("backward", 2), ("result", 8),
    ("hidden", 2), ("mixed", 2), ("pair", 8), ("own_hidden", 2), ("own_mixed", 2), ("own_x", 2), ("own_y", 2), ("own_grad", 2),
    ("other_hidden", 2), ("other_active", 2), ("other_slope", 2),
)


def pipeline_kernel(
    shape_ref, canvas_ref, ograd_ref, kept_ref, cond_ref, bias_ref, w1_hbm, w2_hbm, wm_hbm,
    hidden_own, hidden_other, mixed_own, mixed_other, x_own, y_own, grad_own, active_other, slope_other, window_out, packed_out,
    w1, w2, rows, packs, packs_kept, quarters, grads, up, base, hidden, big, branch, outs, picked, landed, back, bgs, parts, acc, up_mixed, hidden2, extra, mod,
    small, send, arrive, go,
):
    dp, section = lax.axis_index("dp"), lax.axis_index("section")
    high = dp // 16
    partner = ((dp + 16) % 32, section)
    copies = Copies(send, arrive)
    for key, count in PIPE_COPIES:
        copies.name(key, count)
    is_feed = section % 2 == 1

    def load_wm(j):
        return copies.local("wm", j, wm_hbm.at[:, pl.ds(j * D, D)], w2.at[j // 2, pl.ds(j % 2 * D, D)])

    def load_w1(j):
        return copies.local("w1", j, w1_hbm.at[:, pl.ds(j * HALF, HALF)], w1.at[j])

    def load_w2(j):
        return copies.local("w2", j, w2_hbm.at[pl.ds(j * HALF, HALF), :], w2.at[j])

    barrier = pltpu.get_barrier_semaphore()
    for by in (1, 2, 3):
        pl.semaphore_signal(barrier, inc=1, device_id=(dp, (section + by) % 4), device_id_type=MESH)
    pl.semaphore_signal(barrier, inc=1, device_id=partner, device_id_type=MESH)

    for j in range(3):
        load_wm(j).start()
    for j in range(2):
        load_w1(j).start()

    shift = shift_matrix(section)

    def pack(source, c):
        return mm(mm(slots_of_tokens(shape_ref[c]), source[c], NT).astype(BF), shift).astype(BF)

    def send_in(c):
        return copies.remote("in", c * 4 + section, packs.at[0, c], quarters.at[c, section], (dp, 0), c * 4)

    def og_copy(c, s, target):
        if target == 3:
            source, landing = packs_kept.at[c], grads.at[c, s, pl.ds(0, KEPT)]
        else:
            source, landing = packs.at[1, c], grads.at[c, s]
        return copies.remote("og", c * 4 + s, source, landing, (dp, target), 8 + c * 4 + target)

    def take_in(c, s):
        return copies.remote("in", c * 4 + s, packs.at[0, c], quarters.at[c, s], (dp, 0), c * 4)

    packs[0, 0] = pack(canvas_ref, 0)
    pl.semaphore_wait(barrier, 4)

    @pl.when(section != 0)
    def _():
        send_in(0).start()

    packs[0, 1] = pack(canvas_ref, 1)

    @pl.when(section >= 2)
    def _():
        send_in(0).wait_send()

    @pl.when(section != 0)
    def _():
        send_in(1).start()

    for c in range(2):
        low = pack(ograd_ref, c)
        packs[1, c] = low
        packs_kept[c] = pick_kept(low, kept_ref[c : c + 1, :])

    cond = cond_ref[...].astype(F32)
    signal = (cond * (1.0 / (1.0 + jnp.exp(-cond)))).astype(BF)
    small[...] = jnp.zeros_like(small)
    for c in range(2):
        for i in range(9):
            small[54 + c * 9 + i : 55 + c * 9 + i, :] = signal[c : c + 1, i * 128 : (i + 1) * 128].astype(F32)
    for j in range(3):
        load_wm(j).wait()
        part = mm(signal, w2[j // 2, j % 2 * D : (j % 2 + 1) * D]) + bias_ref[:, j * D : (j + 1) * D]
        for c in range(2):
            mod[c, j : j + 1, :] = part[c : c + 1, :]

    @pl.when(is_feed)
    def _():
        for j in range(2):
            load_w2(j).start()

    @pl.when(section >= 2)
    def _():
        send_in(1).wait_send()

    for target in (3, 1):
        for c in range(2):

            @pl.when(section != target)
            def _():
                og_copy(c, section, target).start()

    for j in range(2):
        load_w1(j).wait()

    def shift_of(c):
        return mod[c, 0:1, :]

    def scale_of(c):
        return mod[c, 1:2, :]

    def gate_of(c):
        return mod[c, 2:3, :]

    def put_sums(c, which, value):
        for i in range(9):
            small[pl.ds(c * 27 + which * 9 + i, 1), :] = value[:, i * 128 : (i + 1) * 128]

    def join(parts_ref, c, r, own, target):
        tiles = {}
        for q in range(4):
            value = own if q == target else parts_ref[c, q, part(r)]
            for t in range(3):
                tile = value[:, t * 128 : (t + 1) * 128]
                at = 2 * q + t
                tiles[at] = tile if at not in tiles else tiles[at] + tile
        return jnp.concatenate([tiles[t] for t in range(9)], axis=1)

    def part(r):
        return pl.ds(0, r)

    def send_forward(c, r, source):
        return copies.remote("forward", c, source.at[c, part(r)], rows.at[c, part(r)], (dp, (section + 1) % 4))

    def send_backward(c, r):
        return copies.remote("backward", c, back.at[c, part(r)], up.at[c, part(r)], (dp, (section + 3) % 4))

    def send_done(c):
        return copies.remote("done", c, picked.at[c], landed.at[c], (dp, 1))

    def send_hidden(c, r):
        return copies.remote("hidden", c, hidden.at[c, part(r)], hidden2.at[c, part(r)], partner)

    def keep_hidden(c, r):
        return copies.local("own_hidden", c, hidden.at[c, part(r)], hidden_own.at[c, part(r)])

    def send_mixed(c, r, source, at):
        return copies.remote("mixed", c, source.at[at, part(r)], mixed_other.at[c, part(r)], partner)

    def keep_mixed(c, r, source, at):
        return copies.local("own_mixed", c, source.at[at, part(r)], mixed_own.at[c, part(r)])

    def keep_x(c, r, at):
        return copies.local("own_x", c, big.at[at, part(r)], x_own.at[c, part(r)])

    def keep_y(c, r):
        return copies.local("own_y", c, big.at[4 + c * 2 + high, part(r)], y_own.at[c, part(r)])

    def send_pair(c, k, half, r):
        columns = pl.ds(k * D + (0, EARLY)[half], (EARLY, D - EARLY)[half])
        source = big.at[4 + c * 2 + 1 - high, part(r), columns]
        return copies.remote("pair", (c * 2 + k) * 2 + half, source, y_own.at[c, part(r), columns], partner)

    def mixed_keep(c, r):
        return copies.local("own_mixed", c, big.at[c * 2 + 1, part(r), pl.ds(D, D)], mixed_own.at[c, part(r)])

    def mixed_send(c, r):
        source = big.at[c * 2 + 1, part(r), pl.ds(D, D)]
        return copies.remote("mixed", c, source, mixed_other.at[c, part(r)], partner)

    def keep_grad(c):
        return copies.local("own_grad", c, back.at[c], grad_own.at[c])

    def attend(c, r, live):
        x = rows[c, part(r)].astype(F32)
        hid = norm_forward(x, shift_of(c), scale_of(c))
        hidden[c, part(r)] = hid
        send_hidden(c, r).start()
        keep_hidden(c, r).start()
        big[c * 2, part(r)] = mm(hid, w1[0]).astype(BF)
        big[c * 2 + 1, part(r), 0:D] = mm(hid, w1[1, :, 0:D]).astype(BF)
        bias = None if live is None else key_bias(live, r)
        parts[0, part(r)] = jnp.zeros((r, D), F32)

        def group(g, carry):
            cut = pl.ds(pl.multiple_of(g * 256, 128), WINDOW)
            cut_k = pl.ds(pl.multiple_of(D + g * 256, 128), WINDOW)
            q4 = big[c * 2, part(r), cut]
            k4 = big[c * 2, part(r), cut_k]
            v4 = big[c * 2 + 1, part(r), cut]
            results = []
            for start, offset in HEADS_OF_GROUP:
                side = slice(start, start + 256)
                q = only_head(q4[:, side], offset + 32 * g)
                v = only_head(v4[:, side], offset + 32 * g)
                results.append(mm(softmax_of(q, k4[:, side], bias).astype(BF), v))
            parts[0, part(r), cut] += overlaid(results)
            return carry

        lax.fori_loop(0, 4, group, 0)
        mixed = parts[0, part(r)].astype(BF)
        big[c * 2 + 1, part(r), D:HALF] = mixed
        mixed_keep(c, r).start()
        out = mm(mixed, w1[1, :, D:HALF])
        branch[c, part(r)] = out.astype(BF)
        outs[c, part(r)] = (rows[c, part(r)].astype(F32) + gate_of(c) * out).astype(BF)
        send_forward(c, r, outs).start()

    def attend_back(c, r, live, to_section):
        upstream = up[c, part(r)].astype(F32)
        put_sums(c, 2, jnp.sum(upstream * branch[c, part(r)].astype(F32), axis=0, keepdims=True))
        bg = (upstream * gate_of(c)).astype(BF)
        big[4 + c * 2 + 1, part(r), D:HALF] = bg
        up_mixed[part(r)] = mm(bg, w1[1, :, D:HALF], NT).astype(BF)
        bias = None if live is None else key_bias(live, r)
        parts[:, part(r)] = jnp.zeros((3, r, D), F32)

        def put_parts(low, width):
            cut = pl.ds(low, width)
            big[4 + c * 2, part(r), cut] = (parts[0, part(r), cut] * FACTOR).astype(BF)
            big[4 + c * 2, part(r), pl.ds(D + low, width)] = (parts[1, part(r), cut] * FACTOR).astype(BF)
            big[4 + c * 2 + 1, part(r), cut] = parts[2, part(r), cut].astype(BF)

        def group(g, carry):
            if not to_section:

                @pl.when(g == 2)
                def _():
                    put_parts(0, EARLY)
                    for k in range(2):
                        send_pair(c, k, 0, r).start()

            cut = pl.ds(pl.multiple_of(g * 256, 128), WINDOW)
            cut_k = pl.ds(pl.multiple_of(D + g * 256, 128), WINDOW)
            q4 = big[c * 2, part(r), cut]
            k4 = big[c * 2, part(r), cut_k]
            v4 = big[c * 2 + 1, part(r), cut]
            mg4 = up_mixed[part(r), cut]
            dq, dk, dv = [], [], []
            for start, offset in HEADS_OF_GROUP:
                side = slice(start, start + 256)
                q = only_head(q4[:, side], offset + 32 * g)
                k = only_head(k4[:, side], offset + 32 * g)
                mg = only_head(mg4[:, side], offset + 32 * g)
                soft = softmax_of(q, k, bias)
                soft_grad = mm(mg, v4[:, side], NT)
                dv.append(mm(soft.astype(BF), mg, TN))
                product = soft * soft_grad
                score_grad = (product - soft * jnp.sum(product, axis=-1, keepdims=True)).astype(BF)
                dq.append(mm(score_grad, k))
                dk.append(mm(score_grad, q, TN))
            parts[0, part(r), cut] += overlaid(dq)
            parts[1, part(r), cut] += overlaid(dk)
            parts[2, part(r), cut] += overlaid(dv)
            return carry

        lax.fori_loop(0, 4, group, 0)
        if to_section:
            put_parts(0, EARLY)
        put_parts(EARLY, D - EARLY)
        if not to_section:
            for k in range(2):
                send_pair(c, k, 1, r).start()
        keep_x(c, r, 4 + c * 2 + high).start()
        hidden_grad = mm(big[4 + c * 2, part(r)], w1[0], NT)
        hidden_grad += mm(big[4 + c * 2 + 1, part(r), 0:D], w1[1, :, 0:D], NT)
        grad, shift_grad, scale_grad = norm_backward(
            rows[c, part(r)].astype(F32), scale_of(c), up[c, part(r)].astype(F32), hidden_grad
        )
        back[c, part(r)] = grad
        if to_section:
            send_backward(c, r).start()
        else:
            keep_grad(c).start()
        put_sums(c, 0, shift_grad)
        put_sums(c, 1, scale_grad)

    def exchange_mixed(r):
        for c in range(2):

            @pl.when(high == 0)
            def _():
                mixed_send(c, r).start()

    def finish_attention(r, to_section):
        for c in range(2):
            send_hidden(c, r).wait()
            keep_hidden2(c, r).start()
            keep_hidden(c, r).wait()

            @pl.when(high == 0)
            def _():
                mixed_send(c, r).wait_send()

            @pl.when(high == 1)
            def _():
                mixed_send(c, r).wait_recv()

            mixed_keep(c, r).wait()
            send_forward(c, r, outs).wait_send()
            keep_x(c, r, 4 + c * 2 + high).wait()
            for k in range(2):
                for half in range(2):
                    send_pair(c, k, half, r).wait()
            keep_hidden2(c, r).wait()
            if not to_section:
                keep_grad(c).wait()

    def keep_hidden2(c, r):
        return copies.local("other_hidden", c, hidden2.at[c, part(r)], hidden_other.at[c, part(r)])

    def keep_other(c, r):
        return (
            keep_hidden2(c, r),
            copies.local("other_active", c, extra.at[0, c, part(r)], active_other.at[c, part(r)]),
            copies.local("other_slope", c, extra.at[1, c, part(r)], slope_other.at[c, part(r)]),
        )

    def work_for_partner(c, r):
        active, slope = gelu_pair(mm(hidden2[c, part(r)], w1[high]))
        extra[0, c, part(r)] = active.astype(BF)
        extra[1, c, part(r)] = slope.astype(BF)
        for copy in keep_other(c, r):
            copy.start()

    def send_result(c, q):
        return copies.remote(
            "result", c, outs.at[c, :, pl.ds(256 * q, WINDOW)], window_out.at[c], (dp, q), c * 4 + q
        )

    def keep_result(c):
        return copies.local("result", c * 4 + 1, outs.at[c, :, pl.ds(256, WINDOW)], window_out.at[c])

    @pl.when(section == 0)
    def _():
        def live_of(c):
            lines, width = grid_of(shape_ref[c])
            return lines * width

        def forward(c, carry):
            for s in (1, 2, 3):
                take_in(c, s).wait_recv()
            rows[c] = join(quarters, c, VALID, packs[0, c], 0)
            attend(c, VALID, live_of(c))
            return carry

        def backward(c, carry):
            send_backward(c, VALID).wait_recv()
            attend_back(c, VALID, live_of(c), False)
            return carry

        lax.fori_loop(0, 2, forward, 0)
        pl.semaphore_wait(go, 1)
        exchange_mixed(VALID)
        lax.fori_loop(0, 2, backward, 0)
        finish_attention(VALID, False)

    @pl.when(section == 1)
    def _():
        for j in range(2):
            load_w2(j).wait()

        def forward(c, carry):
            send_forward(c, VALID, outs).wait_recv()
            hid = norm_forward(rows[c].astype(F32), shift_of(c), scale_of(c))
            hidden[c] = hid
            keep_hidden(c, VALID).start()
            for j in range(2):
                active, slope = gelu_pair(mm(hid, w1[j]))
                low = active.astype(BF)
                big[c * 2 + j] = low
                big[4 + c * 2 + j] = slope.astype(BF)
                if j == 0:
                    acc[...] = mm(low, w2[j])
                else:
                    acc[...] += mm(low, w2[j])
            keep_x(c, VALID, c * 2 + high).start()
            out = acc[...]
            branch[c] = out.astype(BF)
            low = (rows[c].astype(F32) + gate_of(c) * out).astype(BF)
            outs[c] = low
            picked[c] = pick_kept(low, kept_ref[pl.ds(c, 1), :])
            send_forward(c, KEPT, picked).start()
            return carry

        lax.fori_loop(0, 2, forward, 0)
        for c in range(2):
            send_forward(c, KEPT, picked).wait_send()
        for c in range(2):
            send_hidden(c, VALID).start()
        for c in range(2):
            for s in (0, 2, 3):
                og_copy(c, s, 1).wait_recv()
            base[c] = join(grads, c, VALID, packs[1, c], 1)
        for c in range(2):
            send_hidden(c, VALID).wait()
        pl.semaphore_signal(go, inc=1, device_id=(dp, 0), device_id_type=MESH)
        for c in range(2):
            work_for_partner(c, VALID)
        for c in range(2):
            send_done(c).wait_recv()
            outs[c] = merge_kept(outs[c], landed[c], kept_ref[c : c + 1, :])
            for q in (0, 2, 3):
                send_result(c, q).start()
            keep_result(c).start()

        def backward(c, carry):
            send_backward(c, KEPT).wait_recv()
            low = merge_kept(base[c], up[c, part(KEPT)], kept_ref[pl.ds(c, 1), :])
            base[c] = low
            upstream = low.astype(F32)
            bg = (upstream * gate_of(c)).astype(BF)
            bgs[c] = bg
            send_mixed(c, VALID, bgs, c).start()
            keep_mixed(c, VALID, bgs, c).start()
            put_sums(c, 2, jnp.sum(upstream * branch[c].astype(F32), axis=0, keepdims=True))
            for j in range(2):
                slope = big[4 + c * 2 + j].astype(F32)
                inner_grad = (mm(bg, w2[j], NT) * slope).astype(BF)
                big[4 + c * 2 + j] = inner_grad
                if j == 0:
                    acc[...] = mm(inner_grad, w1[j], NT)
                else:
                    acc[...] += mm(inner_grad, w1[j], NT)
            keep_y(c, VALID).start()
            grad, shift_grad, scale_grad = norm_backward(
                rows[c].astype(F32), scale_of(c), base[c].astype(F32), acc[...]
            )
            back[c] = grad
            send_backward(c, VALID).start()
            put_sums(c, 0, shift_grad)
            put_sums(c, 1, scale_grad)
            return carry

        lax.fori_loop(0, 2, backward, 0)
        for c in range(2):
            for copy in keep_other(c, VALID):
                copy.wait()
            keep_hidden(c, VALID).wait()
            send_mixed(c, VALID, bgs, c).wait()
            keep_mixed(c, VALID, bgs, c).wait()
            send_backward(c, VALID).wait_send()
            for q in (0, 2, 3):
                send_result(c, q).wait_send()
            keep_result(c).wait()
            keep_x(c, VALID, c * 2 + high).wait()
            keep_y(c, VALID).wait()

    @pl.when(section == 2)
    def _():
        def forward(c, carry):
            send_forward(c, KEPT, outs).wait_recv()
            attend(c, KEPT, None)
            return carry

        def backward(c, carry):
            send_backward(c, KEPT).wait_recv()
            attend_back(c, KEPT, None, True)
            return carry

        lax.fori_loop(0, 2, forward, 0)
        exchange_mixed(KEPT)
        lax.fori_loop(0, 2, backward, 0)
        for c in range(2):
            send_backward(c, KEPT).wait_send()
        for c in range(2):
            for k in range(2):
                for half in range(2):
                    send_pair(c, k, half, KEPT).start()
        finish_attention(KEPT, True)


    @pl.when(section == 3)
    def _():
        for j in range(2):
            load_w2(j).wait()
        for c in range(2):
            for s in (0, 1, 2):
                og_copy(c, s, 3).wait_recv()
            low = join(grads, c, KEPT, packs_kept[c], 3)
            base[c, part(KEPT)] = low
            bg = (low.astype(F32) * gate_of(c)).astype(BF)
            bgs[c, part(KEPT)] = bg
            send_mixed(c, KEPT, bgs, c).start()
            keep_mixed(c, KEPT, bgs, c).start()

        def run(c, carry):
            send_forward(c, KEPT, outs).wait_recv()
            hid = norm_forward(rows[c, part(KEPT)].astype(F32), shift_of(c), scale_of(c))
            hidden[c, part(KEPT)] = hid
            send_hidden(c, KEPT).start()
            keep_hidden(c, KEPT).start()
            bg = bgs[c, part(KEPT)]
            for j in range(2):
                active, slope = gelu_pair(mm(hid, w1[j]))
                low = active.astype(BF)
                inner_grad = (mm(bg, w2[j], NT) * slope).astype(BF)
                big[c * 2 + j, part(KEPT)] = low
                big[4 + c * 2 + j, part(KEPT)] = inner_grad
                ahead, behind = mm(low, w2[j]), mm(inner_grad, w1[j], NT)
                if j == 0:
                    parts[0, part(KEPT)] = ahead
                    parts[1, part(KEPT)] = behind
                else:
                    parts[0, part(KEPT)] += ahead
                    parts[1, part(KEPT)] += behind
            x = rows[c, part(KEPT)].astype(F32)
            upstream = base[c, part(KEPT)].astype(F32)
            grad, shift_grad, scale_grad = norm_backward(x, scale_of(c), upstream, parts[1, part(KEPT)])
            back[c, part(KEPT)] = grad
            send_backward(c, KEPT).start()
            out = parts[0, part(KEPT)]
            picked[c] = (x + gate_of(c) * out).astype(BF)
            send_done(c).start()
            put_sums(c, 0, shift_grad)
            put_sums(c, 1, scale_grad)
            put_sums(c, 2, jnp.sum(upstream * out, axis=0, keepdims=True))
            keep_x(c, KEPT, c * 2 + high).start()
            keep_y(c, KEPT).start()
            return carry

        lax.fori_loop(0, 2, run, 0)
        for c in range(2):
            send_hidden(c, KEPT).wait()
            work_for_partner(c, KEPT)
        for c in range(2):
            for copy in keep_other(c, KEPT):
                copy.wait()
            keep_hidden(c, KEPT).wait()
            send_mixed(c, KEPT, bgs, c).wait()
            keep_mixed(c, KEPT, bgs, c).wait()
            send_backward(c, KEPT).wait_send()
            keep_x(c, KEPT, c * 2 + high).wait()
            keep_y(c, KEPT).wait()
            send_done(c).wait_send()

    @pl.when(section != 1)
    def _():
        for c in range(2):
            send_result(c, 0).wait_recv()

    for c in range(2):

        @pl.when(section == 1)
        def _():
            send_in(c).wait_send()

        for target in (3, 1):

            @pl.when(section != target)
            def _():
                og_copy(c, section, target).wait_send()

    packed_out[...] = small[...].astype(BF)


def pipeline(grid_shape, canvas_in, out_grad, kept_rank, conditioning, bias, w1, w2, wm):
    anywhere = pl.BlockSpec(memory_space=pl.ANY)
    vmem = pl.BlockSpec(memory_space=VMEM)
    canvas = array(2, VALID, D)
    count = sum(n for _, n in PIPE_COPIES)
    return pl.pallas_call(
        pipeline_kernel,
        in_specs=[pl.BlockSpec(memory_space=pltpu.SMEM)] + [vmem] * 5 + [anywhere] * 3,
        out_specs=[anywhere] * 10 + [vmem],
        out_shape=[canvas] * 4
        + [array(2, VALID, HALF)] * 2
        + [canvas]
        + [array(2, VALID, HALF)] * 2
        + [array(2, VALID, WINDOW), array(PACKED, 128)],
        scratch_shapes=[
            VMEM((2, D, HALF), BF),
            VMEM((2, HALF, D), BF),
            VMEM((2, VALID, D), BF),
            VMEM((2, 2, VALID, WINDOW), BF),
            VMEM((2, KEPT, WINDOW), BF),
            VMEM((2, 4, VALID, WINDOW), BF),
            VMEM((2, 4, VALID, WINDOW), BF),
            VMEM((2, VALID, D), BF),
            VMEM((2, VALID, D), BF),
            VMEM((2, VALID, D), BF),
            VMEM((8, VALID, HALF), BF),
            VMEM((2, VALID, D), BF),
            VMEM((2, VALID, D), BF),
            VMEM((2, KEPT, D), BF),
            VMEM((2, KEPT, D), BF),
            VMEM((2, VALID, D), BF),
            VMEM((2, VALID, D), BF),
            VMEM((3, VALID, D), F32),
            VMEM((VALID, D), F32),
            VMEM((VALID, D), BF),
            VMEM((2, VALID, D), BF),
            VMEM((2, 2, VALID, HALF), BF),
            VMEM((2, 3, D), F32),
            VMEM((PACKED, 128), F32),
            pltpu.SemaphoreType.DMA((count,)),
            pltpu.SemaphoreType.DMA((count,)),
            pltpu.SemaphoreType.REGULAR,
        ],
        compiler_params=pltpu.CompilerParams(collective_id=1, has_side_effects=True, vmem_limit_bytes=63 * 2**20),
        cost_estimate=cost(40e9, 60e6),
        name="pipeline",
    )(grid_shape, canvas_in, out_grad, kept_rank, conditioning, bias, w1, w2, wm)


FLOWS = ((0, "y", 0, 640), (0, "z", 640, 512), (1, "y", 0, 512), (1, "z", 512, 640))
CUT = 80
FINAL_COPIES = (
    ("flow", 48), ("left", 8), ("right", 8), ("weights", 1),
    ("gather_y", 6), ("gather_z", 6), ("gather_x", 1), ("window", 8),
)


def final_kernel(
    shape_ref, packed_ref, result_ref, hidden_own, hidden_other, mixed_own, mixed_other, x_own, y_own, grad_own, active_other, slope_other, w2_hbm,
    first_out, second_out, result_out, canvas_out, all_packed,
    left, right, other, w2, sums_first, sums_second, windows_in, *scratch,
):
    count = len(FLOWS)
    ones, twos, threes, sums, tiny1, tiny2, tiny3 = (scratch[i * count : (i + 1) * count] for i in range(7))
    copies = Copies(scratch[7 * count], scratch[7 * count + 1])
    for key, number in FINAL_COPIES:
        copies.name(key, number)
    dp, section = lax.axis_index("dp"), lax.axis_index("section")
    x, z, y = dp // 16, (dp // 4) % 4, dp % 4
    place = {"y": y, "z": z}
    is_odd = section % 2 == 1

    def neighbour(axis, by):
        if axis == "y":
            return (x * 16 + z * 4 + (y + by) % 4, section)
        return (x * 16 + ((z + by) % 4) * 4 + y, section)

    partner = ((dp + 16) % 32, section)
    barrier = pltpu.get_barrier_semaphore()
    for axis in ("y", "z"):
        for by in (1, 2, 3):
            pl.semaphore_signal(barrier, inc=1, device_id=neighbour(axis, by), device_id_type=MESH)
    pl.semaphore_signal(barrier, inc=1, device_id=partner, device_id_type=MESH)

    @pl.when(section != 0)
    def _():
        pl.semaphore_signal(barrier, inc=1, device_id=(dp, 0), device_id_type=MESH)

    def load_left(r, feed):
        result = []
        for c in range(2):
            part, own, theirs = pl.ds(0, r), pl.ds(c * r, r), pl.ds((2 + c) * r, r)
            result.append(copies.local("left", c, x_own.at[c, part], left.at[own]))
            if feed:
                result.append(copies.local("left", 2 + c, active_other.at[c, part], left.at[theirs]))
            else:
                result.append(copies.local("left", 2 + c, y_own.at[c, part], left.at[theirs]))
            result.append(copies.local("right", 4 + c, mixed_own.at[c, part], right.at[1, own]))
            result.append(copies.local("right", 6 + c, mixed_other.at[c, part], right.at[1, theirs]))
        return result

    def load_right(r, feed):
        result = []
        for c in range(2):
            part, own, theirs = pl.ds(0, r), pl.ds(c * r, r), pl.ds((2 + c) * r, r)
            if feed:
                result.append(copies.local("left", 4 + c, y_own.at[c, part], other.at[own]))
                result.append(copies.local("left", 6 + c, slope_other.at[c, part], other.at[theirs]))
            result.append(copies.local("right", c, hidden_own.at[c, part], right.at[0, own]))
            result.append(copies.local("right", 2 + c, hidden_other.at[c, part], right.at[0, theirs]))
        if feed:
            result.append(copies.local("weights", 0, w2_hbm.at[pl.ds(x * HALF, HALF), :], w2))
        return result

    for which, (r, feed) in enumerate(((VALID, False), (VALID, True), (KEPT, False), (KEPT, True))):

        @pl.when(section == which)
        def _():
            for c in load_left(r, feed) + load_right(r, feed):
                c.start()

    all_packed[x, z, y] = packed_ref[...]

    def put(target, k, value):
        target[pl.ds(8 * k, 8)] = value.astype(BF).reshape(8, BLOCK, D)

    def columns(k):
        return pl.ds(pl.multiple_of(k * D, 128), D)

    data = (sums_first, sums_second)
    outs = (first_out, second_out)
    halves = (pl.ds(0, 2), pl.ds(2, 2))
    cuts = (pl.ds(0, CUT), pl.ds(CUT, BLOCK - CUT))

    def axes(flow):
        axis = FLOWS[flow][1]
        return axis, "z" if axis == "y" else "y"

    def step(flow, phase, kind, side, source, target):
        number = ((flow * 2 + phase) * 3 + kind) * 2 + side
        return copies.remote("flow", number, source, target, neighbour(axes(flow)[phase], (1, 3)[side]))

    def block(flow, by, half):
        which, axis, low, width = FLOWS[flow]
        position = (place[axis] + by) % 4
        columns = pl.ds(low, width)
        if axis == "y":
            return [data[which].at[4 * (2 * half + i) + position, :, columns] for i in range(2)]
        return [data[which].at[4 * position + 2 * half + i, :, columns] for i in range(2)]

    def pair_ref(flow, by, half):
        which, axis, low, width = FLOWS[flow]
        position = (place[axis] + by) % 4
        columns = pl.ds(low, width)
        grid = data[which].reshape(4, 4, BLOCK, D)
        if axis == "y":
            return grid.at[pl.ds(2 * half, 2), position, :, columns]
        return grid.at[position, pl.ds(2 * half, 2), :, columns]

    def first_a(flow, side):
        return step(flow, 0, 0, side, pair_ref(flow, 2, side), ones[flow].at[side])

    def first_b(flow, side):
        return step(flow, 0, 1, side, pair_ref(flow, (1, 3)[side], 1 - side), twos[flow].at[side])

    def first_c(flow, side):
        return step(flow, 0, 2, side, ones[flow].at[side], threes[flow].at[side])

    def slab(flow, by, cut):
        return sums[flow].at[(place[axes(flow)[1]] + by) % 4, cut]

    def second_a(flow, side):
        return step(flow, 1, 0, side, slab(flow, 2, cuts[side]), tiny1[flow].at[cuts[side]])

    def second_b(flow, side):
        cut = cuts[1 - side]
        return step(flow, 1, 1, side, slab(flow, (1, 3)[side], cut), tiny2[flow].at[cut])

    def second_c(flow, side):
        return step(flow, 1, 2, side, tiny1[flow].at[cuts[side]], tiny3[flow].at[cuts[side]])

    def begin(flow):
        for side in (0, 1):
            first_a(flow, side).start()
        for side in (0, 1):
            first_b(flow, side).start()

    def forward(flow):
        for side in (0, 1):
            first_a(flow, side).wait()
            own = block(flow, (1, 3)[side], side)
            for i in range(2):
                total = ones[flow][side, i].astype(F32) + own[i][...].astype(F32)
                ones[flow][side, i] = total.astype(BF)
            first_c(flow, side).start()

    def middle(flow):
        for side in (0, 1):
            first_b(flow, side).wait()
            first_c(flow, side).wait()
        for half in (0, 1):
            own = block(flow, 0, half)
            for i in range(2):
                total = own[i][...].astype(F32) + threes[flow][half, i].astype(F32)
                sums[flow][2 * half + i] = (total + twos[flow][1 - half, i].astype(F32)).astype(BF)
        for side in (0, 1):
            second_a(flow, side).start()
        for side in (0, 1):
            second_b(flow, side).start()

    def late(flow):
        for side in (0, 1):
            second_a(flow, side).wait()
            own = slab(flow, (1, 3)[side], cuts[side])[...]
            tiny1[flow][cuts[side]] = (tiny1[flow][cuts[side]].astype(F32) + own.astype(F32)).astype(BF)
            second_c(flow, side).start()

    def finish(flow):
        which, axis, low, width = FLOWS[flow]
        for side in (0, 1):
            second_b(flow, side).wait()
            second_c(flow, side).wait()
        own = sums[flow][place[axes(flow)[1]]].astype(F32)
        outs[which][:, low : low + width] = own + tiny2[flow][...].astype(F32) + tiny3[flow][...].astype(F32)

    even = [i for i, f in enumerate(FLOWS) if f[0] == 0]
    odd = [i for i, f in enumerate(FLOWS) if f[0] == 1]

    def stage(work, flows):
        for flow in flows:
            work(flow)

    def gather(axis, by):
        if axis == "y":
            ref = all_packed.at[x, z, y]
            return copies.remote("gather_y", by - 1, ref, ref, neighbour("y", by), 2 + by)
        if axis == "z":
            ref = all_packed.at[x, z]
            return copies.remote("gather_z", by - 1, ref, ref, neighbour("z", by), 2 + by)
        return copies.remote("gather_x", 0, all_packed.at[x], all_packed.at[x], partner)

    def gathered(axis, by):
        if axis == "y":
            ref = all_packed.at[x, z, (y + 4 - by) % 4]
            return copies.remote("gather_y", by - 1, ref, ref, neighbour("y", by), 2 + by)
        if axis == "z":
            ref = all_packed.at[x, (z + 4 - by) % 4]
            return copies.remote("gather_z", by - 1, ref, ref, neighbour("z", by), 2 + by)
        ref = all_packed.at[1 - x]
        return copies.remote("gather_x", 0, ref, ref, partner)

    def window(c, q):
        source = grad_own.at[c, :, pl.ds(256 * q, WINDOW)]
        return copies.remote("window", c * 4, source, windows_in.at[c], (dp, q), c * 4 + q)

    def own_window(c):
        return copies.local("window", c * 4, grad_own.at[c, :, pl.ds(0, WINDOW)], windows_in.at[c])

    shift = shift_matrix(section)

    def unpack(value, c):
        return mm(mm(value, shift, NT).astype(BF), slots_of_tokens(shape_ref[c]), TN).astype(BF)

    @pl.when(section == 0)
    def _():
        pl.semaphore_wait(barrier, 10)

    @pl.when(section != 0)
    def _():
        pl.semaphore_wait(barrier, 7)

    @pl.when(section == 0)
    def _():
        for c in range(2):
            own_window(c).start()
            for q in (1, 2, 3):
                window(c, q).start()

    for by in (1, 2, 3):
        gather("y", by).start()

    def attention_products(r):
        rows = pl.ds(0, 4 * r)
        for copy in load_left(r, False) + load_right(r, False):
            copy.wait()

        def product(k, carry):
            put(sums_first, k, mm(left[rows, columns(k)], right[x * k, rows], TN))
            return carry

        lax.fori_loop(0, 2, product, 0)
        stage(begin, even)
        second_out[...] = jnp.zeros_like(second_out)

    def feed_products(r):
        rows = pl.ds(0, 4 * r)
        for copy in load_left(r, True):
            copy.wait()

        def second_product(k, carry):
            put(sums_second, k, mm(left[rows, columns(k)], right[1, rows], TN))
            return carry

        def first_product(k, carry):
            put(sums_first, k, mm(other[rows, columns(k)], right[0, rows], TN))

            @pl.when(k == 0)
            def _():
                stage(forward, odd)

            return carry

        lax.fori_loop(0, 2, second_product, 0)
        stage(begin, odd)
        for copy in load_right(r, True):
            copy.wait()

        def inner_gradient(c, carry):
            theirs = pl.ds(pl.multiple_of((2 + c) * r, 128), r)
            active_grad = mm(right[1, theirs], w2[...], NT)
            other[theirs] = (active_grad * other[theirs].astype(F32)).astype(BF)
            return carry

        lax.fori_loop(0, 2, inner_gradient, 0)
        lax.fori_loop(0, 2, first_product, 0)
        stage(begin, even)

    for which, r in ((0, VALID), (2, KEPT)):

        @pl.when(section == which)
        def _():
            attention_products(r)

    for which, r in ((1, VALID), (3, KEPT)):

        @pl.when(section == which)
        def _():
            feed_products(r)

    for by in (1, 2, 3):
        gather("y", by).wait_send()
        gathered("y", by).wait_recv()
    for by in (1, 2, 3):
        gather("z", by).start()

    @pl.when(is_odd)
    def _():
        stage(middle, odd)

    stage(forward, even)
    for by in (1, 2, 3):
        gather("z", by).wait_send()
        gathered("z", by).wait_recv()
    gather("x", 0).start()
    for c in range(2):
        result_out[c] = unpack(result_ref[c], c)
    for work, later in ((middle, late), (late, finish)):

        @pl.when(is_odd)
        def _():
            stage(later, odd)

        stage(work, even)
    stage(finish, even)

    gather("x", 0).wait_send()
    gathered("x", 0).wait_recv()

    for c in range(2):

        @pl.when(section == 0)
        def _():
            own_window(c).wait()
            for q in (1, 2, 3):
                window(c, q).wait_send()

        @pl.when(section != 0)
        def _():
            window(c, 0).wait_recv()

        canvas_out[c] = unpack(windows_in[c], c)


def final(grid_shape, packed, result_window, parts, w2):
    anywhere = pl.BlockSpec(memory_space=pl.ANY)
    vmem = pl.BlockSpec(memory_space=VMEM)
    widths = [f[3] for f in FLOWS]
    pair = [VMEM((2, 2, BLOCK, w), BF) for w in widths]
    tiny = [VMEM((BLOCK, w), BF) for w in widths]
    count = sum(n for _, n in FINAL_COPIES)
    canvas = array(2, QUARTER, SLOTS)
    return pl.pallas_call(
        final_kernel,
        in_specs=[pl.BlockSpec(memory_space=pltpu.SMEM)] + [vmem] * 2 + [anywhere] * 10,
        out_specs=[vmem] * 5,
        out_shape=[array(BLOCK, D, dtype=F32)] * 2 + [canvas] * 2 + [array(2, 4, 4, PACKED, 128)],
        scratch_shapes=[
            VMEM((4 * VALID, HALF), BF),
            VMEM((2, 4 * VALID, D), BF),
            VMEM((4 * VALID, HALF), BF),
            VMEM((HALF, D), BF),
            VMEM((16, BLOCK, D), BF),
            VMEM((16, BLOCK, D), BF),
            VMEM((2, VALID, WINDOW), BF),
        ]
        + pair * 3
        + [VMEM((4, BLOCK, w), BF) for w in widths]
        + tiny * 3
        + [pltpu.SemaphoreType.DMA((count,)), pltpu.SemaphoreType.DMA((count,))],
        compiler_params=pltpu.CompilerParams(collective_id=0, has_side_effects=True, vmem_limit_bytes=63 * 2**20),
        cost_estimate=cost(20e9, 60e6),
        name="final",
    )(grid_shape, packed, result_window, *parts, w2)


def local(
    canvas_in,
    conditioning,
    grid_shape,
    kept_rank,
    first_weight,
    second_weight,
    modulation_weight,
    modulation_bias,
    out_grad,
):
    w1, w2 = first_weight[0], second_weight[0]
    outputs = pipeline(
        grid_shape,
        canvas_in.transpose(0, 2, 1),
        out_grad.transpose(0, 2, 1),
        kept_rank,
        conditioning,
        modulation_bias,
        w1,
        w2,
        modulation_weight[0],
    )
    first_sum, second_sum, result, canvas_grad, packed = final(grid_shape, outputs[10], outputs[9], outputs[:9], w2)
    packed = packed.reshape(32, PACKED, 128)
    all_sums = packed[:, :54].reshape(64, 3 * D)
    all_signal = packed[:, 54:72].reshape(64, D)
    modulation_grad = mm(all_signal, all_sums, TN)
    bias_grad = jnp.sum(all_sums.astype(F32), axis=0)
    return (
        result.transpose(0, 2, 1),
        canvas_grad.transpose(0, 2, 1),
        first_sum.T[None],
        second_sum[None],
        modulation_grad[None],
        bias_grad[None],
    )


def solution(mesh):
    placed = (
        P("dp", None, "section"),
        P("dp", None),
        P("dp"),
        P("dp", None),
        P("section", None, None),
        P("section", None, None),
        P("section", None, None),
        P("section", None),
        P("dp", None, "section"),
    )
    return jax.shard_map(
        local,
        mesh=mesh,
        in_specs=placed,
        out_specs=(
            P("dp", None, "section"),
            P("dp", None, "section"),
            P("section", None, "dp"),
            P("section", "dp", None),
            P("section", None, None),
            P("section", None),
        ),
        check_vma=False,
    )
```

profile of v0, /device:TPU:2, one launch (start us, length us, event | category | flops | bytes accessed | tf_op | source)
XLA Modules:
  0.0 192.0 jit_solution(17136365734001677198)
XLA Ops:
  0.6 130.9 %pipeline.1 = (bf16[2,256,1152]{2,1,0:T(8,128)(2,1)}, bf16[2,256,1152]{2,1,0:T(8,128)(2,1)}, bf16[2,256,1152]{2,1,0:T(8,128)(2,1)}, bf16[2,256,1152]{2,1,0:T(8,1...) custom-call(s32[2]{0:T(128)} %shape_ref.3, ...), custom_call_target="tpu_custom_call" | custom-call | flops 40000000000 | bytes 60000000 | tf_op jit(solution)/shard_map/pipeline/pallas_call | solution.py:734
  131.6 45.2 %final.1 = (f32[144,1152]{1,0:T(8,128)}, f32[144,1152]{1,0:T(8,128)}, bf16[2,288,400]{2,1,0:T(8,128)(2,1)}, bf16[2,288,400]{2,1,0:T(8,128)(2,1)}, bf16[2,4,4,80,128]{4,3,2,1,0:T(8,128)(2,1)}) custom-call(s32[2]{0:T(128)} %shape_ref.3, bf16[80,128]{1,0:T(8,128)(2,1)} %get-tuple-element.22.packed_ref, bf16[2,256,384]{2,1,0:T(8,128)(2,1)} %get-tuple-element.23.result_ref, ...), custom_call_target="tpu_custom_call" | custom-call | flops 20000000000 | bytes 60000000 | tf_op jit(solution)/shard_map/final/pallas_call | solution.py:1120
  176.7 1.0 slice.8
  177.8 0.2 reshape.22
  178.0 1.1 slice.9
  179.0 0.5 reshape.23
  179.5 0.0 copy-start.3
  179.6 0.0 copy-start.2
  179.6 8.1 %convolution_bitcast_fusion = f32[1,1152,3456]{2,1,0:T(8,128)} fusion(bf16[64,1152]{1,0:T(8,128)(2,1)S(1)} %reshape.22, bf16[64,3456]{1,0:T(8,128)(2,1)S(1)} %reshape.23), kind=kOutput, calls=%fused_computation | convolution fusion | flops 509607936 | bytes 16515072 | tf_op jit(solution)/shard_map/dot_general | solution.py:39
  187.7 0.0 copy-start.1
  187.7 0.0 copy-start
  187.7 0.1 convert_reduce_fusion
  187.8 0.6 broadcast_in_dim.15
  188.4 0.0 copy-done.3
  188.4 0.8 copy.19
  189.2 0.0 copy-done.2
  189.2 0.8 copy.20
  190.0 0.0 copy-done.1
  190.0 0.8 copy.21
  190.9 0.0 copy-done
  190.9 0.8 copy.22
Async XLA Ops:
  179.5 8.9 %copy-start.3 = (bf16[2,288,400]{2,1,0:T(8,128)(2,1)S(1)}, bf16[2,288,400]{2,1,0:T(8,128)(2,1)}, u32[]{:S(2)}) copy-start(bf16[2,288,400]{2,1,0:T(8,128)(2,1)} %get-tuple-element.33) | copy-start | bytes 1382404
  179.6 9.7 %copy-start.2 = (bf16[2,288,400]{2,1,0:T(8,128)(2,1)S(1)}, bf16[2,288,400]{2,1,0:T(8,128)(2,1)}, u32[]{:S(2)}) copy-start(bf16[2,288,400]{2,1,0:T(8,128)(2,1)} %get-tuple-element.34) | copy-start | bytes 1382404
  187.7 2.3 %copy-start.1 = (f32[144,1152]{1,0:T(8,128)S(1)}, f32[144,1152]{1,0:T(8,128)}, u32[]{:S(2)}) copy-start(f32[144,1152]{1,0:T(8,128)} %get-tuple-element.35) | copy-start | bytes 1990660
  187.7 3.2 %copy-start = (f32[144,1152]{1,0:T(8,128)S(1)}, f32[144,1152]{1,0:T(8,128)}, u32[]{:S(2)}) copy-start(f32[144,1152]{1,0:T(8,128)} %get-tuple-element.36) | copy-start | bytes 1990660
where the time goes:
time: 195 us; the launch traced here: 192 us
  Pallas kernels  176 us (90%)
  matrix products  8.15 us (4%)
  local copies, waits for them, and re-layouts  6.71 us (3%)
    pallas_call x1, Pallas kernels, pipeline(): pl.pallas_call(pipeline_kernel, in_specs=[pl.BlockSpec(memory_space=pltpu...  131 us
    pallas_call x1, Pallas kernels, final(): pl.pallas_call(final_kernel, in_specs=[pl.BlockSpec(memory_space=pltpu.SM...  45.2 us
    dot_general x1, matrix products, mm(): return lax.dot_general(a, b, dims, preferred_element_type=F32)  8.15 us

commit v1 on v0

--- a/solution.py
+++ b/solution.py
@@ -1141,6 +1141,72 @@
     )(grid_shape, packed, result_window, *parts, w2)
 
 
+STRIPE = 128
+
+
+def closing_kernel(
+    packed_ref, first_ref, second_ref, result_ref, canvas_ref,
+    first_out, second_out, result_out, canvas_out, product_out, bias_out,
+    wide, sums, signals, stage, sems,
+):
+    wide[...] = packed_ref[...].astype(F32)
+
+    def column(row):
+        return wide[pl.ds(row, 32, stride=PACKED), :].astype(BF)
+
+    for c in range(2):
+        lines = pl.ds(32 * c, 32)
+        for t in range(9):
+            signals[lines, t * 128 : (t + 1) * 128] = column(54 + c * 9 + t)
+        for t in range(27):
+            sums[lines, t * 128 : (t + 1) * 128] = column(c * 27 + t)
+    bias_out[...] = jnp.sum(sums[...].astype(F32), axis=0, keepdims=True)
+
+    def write(j):
+        lines = pl.ds(j * STRIPE, STRIPE)
+        return pltpu.make_async_copy(stage.at[j % 3], product_out.at[lines, :], sems.at[j])
+
+    for j in range(D // STRIPE):
+        if j >= 3:
+            write(j - 3).wait()
+        stage[j % 3] = mm(signals[:, j * STRIPE : (j + 1) * STRIPE], sums[...], TN)
+        write(j).start()
+    first_out[...] = first_ref[...]
+    second_out[...] = second_ref[...]
+    result_out[...] = result_ref[...]
+    canvas_out[...] = canvas_ref[...]
+    for j in range(D // STRIPE - 3, D // STRIPE):
+        write(j).wait()
+
+
+def closing(packed, first, second, result, canvas):
+    anywhere = pl.BlockSpec(memory_space=pl.ANY)
+    vmem = pl.BlockSpec(memory_space=VMEM)
+    return pl.pallas_call(
+        closing_kernel,
+        in_specs=[vmem] * 5,
+        out_specs=[vmem] * 4 + [anywhere, vmem],
+        out_shape=[
+            array(*first.shape, dtype=F32),
+            array(*second.shape, dtype=F32),
+            array(*result.shape),
+            array(*canvas.shape),
+            array(D, 3 * D, dtype=F32),
+            array(1, 3 * D, dtype=F32),
+        ],
+        scratch_shapes=[
+            VMEM((32 * PACKED, 128), F32),
+            VMEM((64, 3 * D), BF),
+            VMEM((64, D), BF),
+            VMEM((3, STRIPE, 3 * D), F32),
+            pltpu.SemaphoreType.DMA((D // STRIPE,)),
+        ],
+        compiler_params=pltpu.CompilerParams(vmem_limit_bytes=63 * 2**20),
+        cost_estimate=cost(2 * 64 * D * 3 * D, 4 * D * 3 * D),
+        name="closing",
+    )(packed, first, second, result, canvas)
+
+
 def local(
     canvas_in,
     conditioning,
@@ -1165,18 +1231,16 @@
         modulation_weight[0],
     )
     first_sum, second_sum, result, canvas_grad, packed = final(grid_shape, outputs[10], outputs[9], outputs[:9], w2)
-    packed = packed.reshape(32, PACKED, 128)
-    all_sums = packed[:, :54].reshape(64, 3 * D)
-    all_signal = packed[:, 54:72].reshape(64, D)
-    modulation_grad = mm(all_signal, all_sums, TN)
-    bias_grad = jnp.sum(all_sums.astype(F32), axis=0)
+    first_sum, second_sum, result, canvas_grad, modulation_grad, bias_grad = closing(
+        packed.reshape(32 * PACKED, 128), first_sum, second_sum, result, canvas_grad
+    )
     return (
         result.transpose(0, 2, 1),
         canvas_grad.transpose(0, 2, 1),
         first_sum.T[None],
         second_sum[None],
         modulation_grad[None],
-        bias_grad[None],
+        bias_grad,
     )
 
 

time: 195 us -> 190 us (0.974)
  Pallas kernels: 176 us -> 186 us
  matrix products: 8.15 us -> 0 us
  local copies, waits for them, and re-layouts: 6.71 us -> 0 us
    pallas_call x0 -> x1, Pallas kernels: none -> 9.87 us  [closing(): pl.pallas_call(closing_kernel, in_specs=[vmem] * 5, out_specs=[vmem] * 4...]
    dot_general x1 -> x0, matrix products: 8.15 us -> none  [mm(): return lax.dot_general(a, b, dims, preferred_element_type=F32)]
    unnamed x12 -> x0, local copies, waits for them, and re-layouts: 3.32 us -> none
    slice x2 -> x0, local copies, waits for them, and re-layouts: 2.08 us -> none  [the longest x1 1.06 us: local(): all_sums = packed[:, :54].reshape(64, 3 * D)]
where the time goes in v1:
time: 190 us; the launch traced here: 187 us
  Pallas kernels  186 us (98%)
    pallas_call x1, Pallas kernels, pipeline(): pl.pallas_call(pipeline_kernel, in_specs=[pl.BlockSpec(memory_space=pltpu...  131 us
    pallas_call x1, Pallas kernels, final(): pl.pallas_call(final_kernel, in_specs=[pl.BlockSpec(memory_space=pltpu.SM...  45.1 us
    pallas_call x1, Pallas kernels, closing(): pl.pallas_call(closing_kernel, in_specs=[vmem] * 5, out_specs=[vmem] * 4...  9.87 us

profile of v1, /device:TPU:2, one launch (start us, length us, event | category | flops | bytes accessed | tf_op | source)
XLA Modules:
  0.0 186.9 jit_solution(7284034818859638789)
XLA Ops:
  0.6 130.9 %pipeline.1 = (bf16[2,256,1152]{2,1,0:T(8,128)(2,1)}, bf16[2,256,1152]{2,1,0:T(8,128)(2,1)}, bf16[2,256,1152]{2,1,0:T(8,128)(2,1)}, bf16[2,256,1152]{2,1,0:T(8,1...) custom-call(s32[2]{0:T(128)} %shape_ref.3, ...), custom_call_target="tpu_custom_call" | custom-call | flops 40000000000 | bytes 60000000 | tf_op jit(solution)/shard_map/pipeline/pallas_call | solution.py:734
  131.6 45.1 %final.1 = (f32[144,1152]{1,0:T(8,128)}, f32[144,1152]{1,0:T(8,128)}, bf16[2,288,400]{2,1,0:T(8,128)(2,1)}, bf16[2,288,400]{2,1,0:T(8,128)(2,1)}, bf16[2,4,4,80,128]{4,3,2,1,0:T(8,128)(2,1)}) custom-call(s32[2]{0:T(128)} %shape_ref.3, bf16[80,128]{1,0:T(8,128)(2,1)} %get-tuple-element.28.packed_ref, bf16[2,256,384]{2,1,0:T(8,128)(2,1)} %get-tuple-element.29.result_ref, ...), custom_call_target="tpu_custom_call" | custom-call | flops 20000000000 | bytes 60000000 | tf_op jit(solution)/shard_map/final/pallas_call | solution.py:1120
  176.7 9.9 %closing.1 = (f32[144,1152]{1,0:T(8,128)}, f32[144,1152]{1,0:T(8,128)}, bf16[2,288,400]{2,1,0:T(8,128)(2,1)}, bf16[2,288,400]{2,1,0:T(8,128)(2,1)}, f32[1152,3456]{1,0:T(8,128)}, /*index=5*/f32[1,3456]{1,0:T(1,128)}) custom-call(bf16[2560,128]{1,0:T(8,128)(2,1)} %bitcast.13, f32[144,1152]{1,0:T(8,128)} %get-tuple-element.40.first_ref, ...), custom_call_target="tpu_custom_call" | custom-call | flops 509607936 | bytes 15925248 | tf_op jit(solution)/shard_map/closing/pallas_call | solution.py:1185

commit v2 on v1

--- a/solution.py
+++ b/solution.py
@@ -19,7 +19,7 @@
 QUARTER = D // 4
 WINDOW = 384
 PACKED = 80
-EARLY = 512
+PIECES = ((0, 256), (256, 256), (512, 256), (768, 384))
 HEAD = D // HEADS
 BLOCK = FF // 32
 EPSILON = 1e-06
@@ -166,7 +166,7 @@
 
 PIPE_COPIES = (
     ("wm", 3), ("w1", 2), ("w2", 2), ("in", 8), ("og", 16), ("forward", 2), ("done", 2), ("backward", 2), ("result", 8),
-    ("hidden", 2), ("mixed", 2), ("pair", 8), ("own_hidden", 2), ("own_mixed", 2), ("own_x", 2), ("own_y", 2), ("own_grad", 2),
+    ("hidden", 2), ("mixed", 2), ("pair", 16), ("own_hidden", 2), ("own_mixed", 2), ("own_x", 2), ("own_y", 2), ("own_grad", 2),
     ("other_hidden", 2), ("other_active", 2), ("other_slope", 2),
 )
 
@@ -328,10 +328,10 @@
     def keep_y(c, r):
         return copies.local("own_y", c, big.at[4 + c * 2 + high, part(r)], y_own.at[c, part(r)])
 
-    def send_pair(c, k, half, r):
-        columns = pl.ds(k * D + (0, EARLY)[half], (EARLY, D - EARLY)[half])
+    def send_pair(c, k, piece, r):
+        columns = pl.ds(k * D + PIECES[piece][0], PIECES[piece][1])
         source = big.at[4 + c * 2 + 1 - high, part(r), columns]
-        return copies.remote("pair", (c * 2 + k) * 2 + half, source, y_own.at[c, part(r), columns], partner)
+        return copies.remote("pair", (c * 2 + k) * 4 + piece, source, y_own.at[c, part(r), columns], partner)
 
     def mixed_keep(c, r):
         return copies.local("own_mixed", c, big.at[c * 2 + 1, part(r), pl.ds(D, D)], mixed_own.at[c, part(r)])
@@ -395,12 +395,13 @@
 
         def group(g, carry):
             if not to_section:
-
-                @pl.when(g == 2)
-                def _():
-                    put_parts(0, EARLY)
-                    for k in range(2):
-                        send_pair(c, k, 0, r).start()
+                for piece in range(3):
+
+                    @pl.when(g == piece + 1)
+                    def _():
+                        put_parts(*PIECES[piece])
+                        for k in range(2):
+                            send_pair(c, k, piece, r).start()
 
             cut = pl.ds(pl.multiple_of(g * 256, 128), WINDOW)
             cut_k = pl.ds(pl.multiple_of(D + g * 256, 128), WINDOW)
@@ -428,11 +429,11 @@
 
         lax.fori_loop(0, 4, group, 0)
         if to_section:
-            put_parts(0, EARLY)
-        put_parts(EARLY, D - EARLY)
+            put_parts(0, PIECES[3][0])
+        put_parts(*PIECES[3])
         if not to_section:
             for k in range(2):
-                send_pair(c, k, 1, r).start()
+                send_pair(c, k, 3, r).start()
         keep_x(c, r, 4 + c * 2 + high).start()
         hidden_grad = mm(big[4 + c * 2, part(r)], w1[0], NT)
         hidden_grad += mm(big[4 + c * 2 + 1, part(r), 0:D], w1[1, :, 0:D], NT)
@@ -472,8 +473,8 @@
             send_forward(c, r, outs).wait_send()
             keep_x(c, r, 4 + c * 2 + high).wait()
             for k in range(2):
-                for half in range(2):
-                    send_pair(c, k, half, r).wait()
+                for piece in range(4):
+                    send_pair(c, k, piece, r).wait()
             keep_hidden2(c, r).wait()
             if not to_section:
                 keep_grad(c).wait()
@@ -637,8 +638,8 @@
             send_backward(c, KEPT).wait_send()
         for c in range(2):
             for k in range(2):
-                for half in range(2):
-                    send_pair(c, k, half, KEPT).start()
+                for piece in range(4):
+                    send_pair(c, k, piece, KEPT).start()
         finish_attention(KEPT, True)
 
 
@@ -1082,6 +1083,13 @@
     gather("x", 0).start()
     for c in range(2):
         result_out[c] = unpack(result_ref[c], c)
+
+    @pl.when(section == 0)
+    def _():
+        for c in range(2):
+            own_window(c).wait()
+            canvas_out[c] = unpack(windows_in[c], c)
+
     for work, later in ((middle, late), (late, finish)):
 
         @pl.when(is_odd)
@@ -1098,15 +1106,13 @@
 
         @pl.when(section == 0)
         def _():
-            own_window(c).wait()
             for q in (1, 2, 3):
                 window(c, q).wait_send()
 
         @pl.when(section != 0)
         def _():
             window(c, 0).wait_recv()
-
-        canvas_out[c] = unpack(windows_in[c], c)
+            canvas_out[c] = unpack(windows_in[c], c)
 
 
 def final(grid_shape, packed, result_window, parts, w2):

time: 190 us -> 190 us (level)
  no operation moved by 1% of the time
where the time goes in v2:
time: 190 us; the launch traced here: 187 us
  Pallas kernels  186 us (98%)
    pallas_call x1, Pallas kernels, pipeline(): pl.pallas_call(pipeline_kernel, in_specs=[pl.BlockSpec(memory_space=pltpu...  131 us
    pallas_call x1, Pallas kernels, final(): pl.pallas_call(final_kernel, in_specs=[pl.BlockSpec(memory_space=pltpu.SM...  45 us
    pallas_call x1, Pallas kernels, closing(): pl.pallas_call(closing_kernel, in_specs=[vmem] * 5, out_specs=[vmem] * 4...  9.86 us

profile of v2, /device:TPU:2, one launch (start us, length us, event | category | flops | bytes accessed | tf_op | source)
XLA Modules:
  0.0 186.9 jit_solution(12652294014507815793)
XLA Ops:
  0.6 131.1 %pipeline.1 = (bf16[2,256,1152]{2,1,0:T(8,128)(2,1)}, bf16[2,256,1152]{2,1,0:T(8,128)(2,1)}, bf16[2,256,1152]{2,1,0:T(8,128)(2,1)}, bf16[2,256,1152]{2,1,0:T(8,1...) custom-call(s32[2]{0:T(128)} %shape_ref.3, ...), custom_call_target="tpu_custom_call" | custom-call | flops 40000000000 | bytes 60000000 | tf_op jit(solution)/shard_map/pipeline/pallas_call | solution.py:735
  131.8 45.0 %final.1 = (f32[144,1152]{1,0:T(8,128)}, f32[144,1152]{1,0:T(8,128)}, bf16[2,288,400]{2,1,0:T(8,128)(2,1)}, bf16[2,288,400]{2,1,0:T(8,128)(2,1)}, bf16[2,4,4,80,128]{4,3,2,1,0:T(8,128)(2,1)}) custom-call(s32[2]{0:T(128)} %shape_ref.3, bf16[80,128]{1,0:T(8,128)(2,1)} %get-tuple-element.28.packed_ref, bf16[2,256,384]{2,1,0:T(8,128)(2,1)} %get-tuple-element.29.result_ref, ...), custom_call_target="tpu_custom_call" | custom-call | flops 20000000000 | bytes 60000000 | tf_op jit(solution)/shard_map/final/pallas_call | solution.py:1126
  176.8 9.9 %closing.1 = (f32[144,1152]{1,0:T(8,128)}, f32[144,1152]{1,0:T(8,128)}, bf16[2,288,400]{2,1,0:T(8,128)(2,1)}, bf16[2,288,400]{2,1,0:T(8,128)(2,1)}, f32[1152,3456]{1,0:T(8,128)}, /*index=5*/f32[1,3456]{1,0:T(1,128)}) custom-call(bf16[2560,128]{1,0:T(8,128)(2,1)} %bitcast.13, f32[144,1152]{1,0:T(8,128)} %get-tuple-element.40.first_ref, ...), custom_call_target="tpu_custom_call" | custom-call | flops 509607936 | bytes 15925248 | tf_op jit(solution)/shard_map/closing/pallas_call | solution.py:1191
